TPU v7x, 512 devices: a whole 4x8x8 slice. The times are simulated.
512 devices in a mesh: row: 32 (over y, x), col: 16 (over z, core).
Axes of the slice: x: 4, y: 8, z: 8, core: 2. Of those that a mesh axis runs over, the one named last changes fastest.
Arguments:
- sequence_features: bfloat16 [128, 1024, 64], P(None, ('row', 'col')), may hold values from -6 to 6
- standardize_scale: float32 [64], replicated, may hold values from 0.1 to 1.9
- standardize_shift: float32 [64], replicated, may hold values from -3 to 3
- first_projection_kernel: bfloat16 [64, 32], replicated, may hold values from -0.75 to 0.75
- first_projection_shift: float32 [32], replicated, may hold values from -3 to 3
- second_projection_kernel: bfloat16 [64, 32], replicated, may hold values from -0.75 to 0.75
- second_projection_shift: float32 [32], replicated, may hold values from -3 to 3
- final_projection_kernel: bfloat16 [1024, 128], replicated, may hold values from -2 to 2
- final_projection_shift: float32 [128], replicated, may hold values from -3 to 3
- cross_molecule_shift: float32 [128], replicated, may hold values from -3 to 3
- residue_molecule_label: int32 [1024], replicated, may hold values from 0 to 3, never falling along the last dimension, each value on 1 to 512 neighbouring positions
- selected_tile_couples: int32 [16, 2], replicated, may hold values from 0 to 7, as said below
- result_adjoint: bfloat16 [1024, 1024, 128], P('row', 'col'), may hold values from -6 to 6
Outputs:
- pair_out: bfloat16 [1024, 1024, 128], P('row', 'col')
- left_grad: float32 [128, 1024, 32], P(None, ('row', 'col'))
- right_grad: float32 [128, 1024, 32], P(None, ('col', 'row'))
Inputs may be any that keep to these rules, and one draw needn't show every extreme that they name: `selected_tile_couples`: pairs are distinct; every diagonal pair (k, k) for k below 8 is listed. `residue_molecule_label`: never falls along the tokens.
All inputs are finite; a program needn't handle non-finite values.
Results may differ from a plain program's by a relative error of at most 0.0057.
Values may be sent and summed in bfloat16 or wider, within the bound.
A program may use at most 64 MiB of HBM per device.

v0:
```python
import jax
import jax.numpy as jnp
from jax import lax
from jax.sharding import PartitionSpec as P

BLK = 128
RB = 8


def from_root(array, axis, root):
    mine = lax.axis_index(axis) == root
    return lax.psum(jnp.where(mine, array, jnp.zeros_like(array)), axis)


def standardize_features(sequence_features, standardize_scale, standardize_shift):
    result_entries = sequence_features.astype(jnp.float32)
    mean = jnp.mean(result_entries, axis=-1, keepdims=True)
    var = jnp.mean((result_entries - mean) ** 2, axis=-1, keepdims=True)
    return (
        (result_entries - mean) * lax.rsqrt(var + 1e-05) * standardize_scale + standardize_shift
    ).astype(jnp.bfloat16)


def project(standardized_features, weight, bias):
    mixed = jnp.einsum(
        "slc,cf->slf", standardized_features, weight, preferred_element_type=jnp.float32
    )
    return (mixed + bias).astype(jnp.bfloat16)


def per_device(
    sequence_features,
    standardize_scale,
    standardize_shift,
    first_projection_kernel,
    first_projection_shift,
    second_projection_kernel,
    second_projection_shift,
    final_projection_kernel,
    final_projection_shift,
    cross_molecule_shift,
    residue_molecule_label,
    selected_tile_couples,
    result_adjoint,
):
    standardized_features = standardize_features(
        sequence_features, standardize_scale, standardize_shift
    )
    left_own = project(standardized_features, first_projection_kernel, first_projection_shift)
    right_own = project(standardized_features, second_projection_kernel, second_projection_shift)
    left_factor_rows, right_rows = (
        lax.all_gather(left_own, "col", axis=1, tiled=True),
        lax.all_gather(right_own, "col", axis=1, tiled=True),
    )
    ratio = lax.axis_size("row") // lax.axis_size("col")
    row_id = lax.axis_index("row")
    col_id = lax.axis_index("col")
    alignment_rows = left_factor_rows.shape[0]
    block_row_tokens = left_factor_rows.shape[1]
    block_column_tokens = block_row_tokens * ratio
    factor_matrix = left_factor_rows.shape[2]
    pair_width = final_projection_kernel.shape[1]
    pieces = [from_root(right_rows, "row", col_id * ratio + step) for step in range(ratio)]
    right_cols = jnp.concatenate(pieces, axis=1)
    row_tokens = row_id * block_row_tokens + jnp.arange(block_row_tokens, dtype=jnp.int32)
    col_tokens = col_id * block_column_tokens + jnp.arange(block_column_tokens, dtype=jnp.int32)
    row_hits = (row_tokens[:, None] // BLK == selected_tile_couples[None, :, 0]).astype(jnp.float32)
    col_hits = (col_tokens[:, None] // BLK == selected_tile_couples[None, :, 1]).astype(jnp.float32)
    listed = jnp.dot(row_hits, col_hits.T, precision=lax.Precision.HIGHEST)
    chain_rows = lax.dynamic_slice_in_dim(
        residue_molecule_label, row_id * block_row_tokens, block_row_tokens, 0
    )
    chain_cols = lax.dynamic_slice_in_dim(
        residue_molecule_label, col_id * block_column_tokens, block_column_tokens, 0
    )
    apart = (chain_rows[:, None] != chain_cols[None, :]).astype(jnp.float32)
    steps_count = block_row_tokens // RB

    def row_step(right_acc, index):
        start = index * RB
        left_blk = lax.dynamic_slice_in_dim(left_factor_rows, start, RB, 1)
        keep = lax.dynamic_slice_in_dim(listed, start, RB, 0)[:, :, None]
        apart_blk = lax.dynamic_slice_in_dim(apart, start, RB, 0)[:, :, None]
        outer = (
            jnp.einsum("sic,sje->ijce", left_blk, right_cols, preferred_element_type=jnp.float32)
            / alignment_rows
        )
        outer = outer.astype(jnp.bfloat16).reshape(
            RB * block_column_tokens, factor_matrix * factor_matrix
        )
        value = jnp.dot(outer, final_projection_kernel, preferred_element_type=jnp.float32).reshape(
            RB, block_column_tokens, pair_width
        )
        value = ((value + final_projection_shift + cross_molecule_shift * apart_blk) * keep).astype(
            jnp.bfloat16
        )
        cotangent = lax.dynamic_slice_in_dim(result_adjoint, start, RB, 0).reshape(
            RB * block_column_tokens, pair_width
        )
        outer_grad = lax.dot_general(
            cotangent,
            final_projection_kernel,
            (((1,), (1,)), ((), ())),
            preferred_element_type=jnp.float32,
        )
        outer_grad = (
            outer_grad.reshape(RB, block_column_tokens, factor_matrix * factor_matrix) * keep
        ).astype(jnp.bfloat16)
        outer_grad = outer_grad.reshape(RB, block_column_tokens, factor_matrix, factor_matrix)
        delta_left = (
            jnp.einsum("ijce,sje->sic", outer_grad, right_cols, preferred_element_type=jnp.float32)
            / alignment_rows
        )
        delta_right = (
            jnp.einsum("ijce,sic->sje", outer_grad, left_blk, preferred_element_type=jnp.float32)
            / alignment_rows
        )
        return (right_acc + delta_right, (value, delta_left))

    initial_carry = jnp.zeros((alignment_rows, block_column_tokens, factor_matrix), jnp.float32)
    right_acc, (result_entries, factor_cotangents) = lax.scan(
        row_step, initial_carry, jnp.arange(steps_count, dtype=jnp.int32)
    )
    pair_tile = result_entries.reshape(block_row_tokens, block_column_tokens, pair_width)
    left_accumulator = jnp.transpose(factor_cotangents, (1, 0, 2, 3)).reshape(
        alignment_rows, block_row_tokens, factor_matrix
    )
    pair_tile, left_accumulator, right_acc = (pair_tile, left_accumulator, right_acc)
    left_grad = lax.psum_scatter(left_accumulator, "col", scatter_dimension=1, tiled=True)
    right_grad = lax.psum_scatter(right_acc, "row", scatter_dimension=1, tiled=True)
    return (pair_tile, left_grad, right_grad)


def solution(mesh):
    placed = (
        P(None, ("row", "col"), None),
        P(),
        P(),
        P(),
        P(),
        P(),
        P(),
        P(),
        P(),
        P(),
        P(),
        P(),
        P("row", "col", None),
    )
    return jax.shard_map(
        per_device,
        mesh=mesh,
        in_specs=placed,
        out_specs=(
            P("row", "col", None),
            P(None, ("row", "col"), None),
            P(None, ("col", "row"), None),
        ),
        check_vma=False,
    )
```

profile of v0, /device:TPU:1, one launch (start us, length us, event | category | flops | bytes accessed | tf_op | source)
XLA Modules:
  0.0 530.4 jit_solution(5860275097616158377)
XLA Ops:
  9.8 25.2 %all_gather.7 = bf16[128,32,32]{0,2,1:T(8,128)(2,1)S(1)} all-gather(bf16[128,2,32]{0,2,1:T(8,128)(2,1)S(1)} %fusion.44), channel_id=1, replica_groups=mesh['row'=32,'col'=16] {'col'}, dimensions={1}, use_global_device_ids=true | all-gather | bytes 278528 | tf_op jit(solution)/shard_map/all_gather | solution.py:53
  39.2 16.6 %all_gather.6 = bf16[128,32,32]{0,2,1:T(8,128)(2,1)} all-gather(bf16[128,2,32]{0,2,1:T(8,128)(2,1)S(1)} %fusion.43), channel_id=1, replica_groups=mesh['row'=32,'col'=16] {'col'}, dimensions={1}, use_global_device_ids=true | all-gather | bytes 278528 | tf_op jit(solution)/shard_map/all_gather | solution.py:52
  56.1 130.4 %all-reduce.3.cloned.1.call-done = (bf16[128,32,32]{0,2,1:T(8,128)(2,1)}, bf16[128,32,32]{0,2,1:T(8,128)(2,1)}) async-done(((bf16[128,32,32]{0,2,1:T(8,128)(2,1)}, bf16[128,32,32]{0,2,1:T(8,128)(2,1)}), (bf16[128,32,32]{0,2,1:T(8,128)(2,1)}, bf16[128,32,32]{0,2,1:T(8,128)(2,1)})) %all-reduce.3.cloned.1.call-update) | async-done | bytes 524304 | tf_op jit(solution)/shard_map/psum | solution.py:12
  188.6 56.0 %while.15 = (s32[]{:T(128)}, f32[128,64,32]{0,1,2:T(8,128)}, bf16[4,8,64,128]{3,2,1,0:T(8,128)(2,1)}, f32[4,128,8,32]{1,3,2,0:T(8,128)}, s32[4]{0:T(128)S(1)}, /...) while((s32[]{:T(128)}, f32[128,64,32]{0,1,2:T(8,128)}, ...), condition=%wide.region_5.6_spmd.clone, body=%wide.region_4.5_spmd.clone.sunk | while | flops 674332672 | bytes 13648113 | solution.py:121
  189.9 1.8 fusion.88
  192.5 1.4 fusion.89
  194.0 1.3 multiply_convert_fusion.3
  196.4 2.7 fusion.87
  199.1 3.2 fusion.90
  203.6 1.8 fusion.88
  206.2 1.4 fusion.89
  210.1 3.2 fusion.87
  213.3 3.2 fusion.90
  217.7 1.8 fusion.88
  220.3 1.4 fusion.89
  224.2 3.2 fusion.87
  227.4 3.2 fusion.90
  231.8 1.8 fusion.88
  234.4 1.4 fusion.89
  238.3 3.2 fusion.87
  241.5 3.2 fusion.90
  244.7 2.8 copy.33
  247.6 56.1 %reduce-scatter.3.cloned.1.call-done = f32[128,2,32]{0,2,1:T(8,128)} async-done(((f32[128,32,32]{0,2,1:T(8,128)}), f32[128,2,32]{0,2,1:T(8,128)}) %reduce-scatter.3.cloned.1.call-update) | async-done | bytes 32784 | tf_op jit(solution)/shard_map/reduce_scatter | solution.py:129
  303.7 220.2 %reduce-scatter.5.cloned.1.call-done = f32[128,2,32]{0,2,1:T(8,128)} async-done(((f32[128,64,32]{0,2,1:T(8,128)}), f32[128,2,32]{0,2,1:T(8,128)}) %reduce-scatter.5.cloned.1.call-update) | async-done | bytes 32784 | tf_op jit(solution)/shard_map/reduce_scatter | solution.py:130
  (53 shorter events, 23.2 us)
Async XLA Ops:
  7.2 1.7 copy-start
  7.2 179.3 %all-reduce.3.cloned.1.call-start = ((), (), s32[]{:S(2)}) async-start(), calls=%async_computation.4 | async-start | bytes 1048576 | tf_op jit(solution)/shard_map/psum | solution.py:12
  35.0 153.6 %copy-start.1 = (bf16[1024,128]{1,0:T(8,128)(2,1)S(1)}, bf16[1024,128]{1,0:T(8,128)(2,1)}, u32[]{:S(2)}) copy-start(bf16[1024,128]{1,0:T(8,128)(2,1)} %param.22) | copy-start | bytes 786436
  35.0 153.6 %copy-start.2 = (f32[128]{0:T(128)S(1)}, f32[128]{0:T(128)}, u32[]{:S(2)}) copy-start(f32[128]{0:T(128)} %param.23) | copy-start | bytes 1540
  35.0 153.6 %copy-start.3 = (f32[128]{0:T(128)S(1)}, f32[128]{0:T(128)}, u32[]{:S(2)}) copy-start(f32[128]{0:T(128)} %param.24) | copy-start | bytes 1540
  35.9 267.8 %reduce-scatter.3.cloned.1.call-start = ((), (), s32[]{:S(2)}) async-start(), calls=%async_computation.2 | async-start | bytes 557056 | tf_op jit(solution)/shard_map/reduce_scatter | solution.py:129
  244.7 279.2 %reduce-scatter.5.cloned.1.call-start = ((), (), s32[]{:S(2)}) async-start(), calls=%async_computation.3 | async-start | bytes 1081344 | tf_op jit(solution)/shard_map/reduce_scatter | solution.py:130
Sparse Core Ops, SparseCore 0:
  36.0 150.4 all-reduce.2
  244.8 58.8 reduce-scatter.2
  308.7 215.1 reduce-scatter.4
where the time goes:
time: 535 us; the launch traced here: 530 us
  waiting for transfers between devices  407 us (76%)
  matrix products  45.4 us (8%)
  blocking collectives  41.7 us (8%)
  local copies, waits for them, and re-layouts  16.1 us (3%)
  between operations  13.8 us (3%)
    reduce_scatter x1, waiting for transfers between devices, per_device(): lax.psum_scatter(right_acc, 'row', scatter_dimension=1, tiled=True)  220 us
    psum x1, waiting for transfers between devices, from_root(): return lax.psum(jnp.where(mine, array, jnp.zeros_like(array)), axis)  130 us
    reduce_scatter x1, waiting for transfers between devices, per_device(): lax.psum_scatter(left_accumulator, 'col', scatter_dimension=1, tiled=True)  56.1 us
    all_gather x1, blocking collectives, per_device(): lax.all_gather(right_own, 'col', axis=1, tiled=True)  25.2 us
    all_gather x1, blocking collectives, per_device(): lax.all_gather(left_own, 'col', axis=1, tiled=True)  16.6 us
    dot_general x4, matrix products, row_step(): jnp.einsum('ijce,sje->sic', outer_grad, right_cols, preferred_element_typ...  12.7 us
    dot_general x4, matrix products, row_step(): jnp.einsum('ijce,sic->sje', outer_grad, left_blk, preferred_element_type=...  12.2 us
  transfers between devices with their start and end apart: 3, of which 3 were waited for; matrix products, arithmetic and copies ran while one was open for 1% of the time, Pallas kernels for 0%

commit v1 on v0

v1 whole, which is shorter than its diff:
```python
import jax
import jax.numpy as jnp
from jax import lax
from jax.experimental import pallas as pl
from jax.experimental.pallas import tpu as pltpu
from jax.sharding import PartitionSpec as P

F32 = jnp.float32
BF16 = jnp.bfloat16
MESH = pl.DeviceIdType.MESH

NX, NY, NZ, NK = 4, 8, 8, 2
NCOL = NZ * NK
S = 128
C = 32
PW = 128
TI = 32
TJ = 64
OWN = 2 * C
G = 4
NG = TI // G
BLK = 128


def place():
    row, col = lax.axis_index("row"), lax.axis_index("col")
    return row, col, row % NX, row // NX, col // NK, col % NK


def remote(src, dst, send, recv, row, col):
    return pltpu.make_async_remote_copy(
        src_ref=src, dst_ref=dst, send_sem=send, recv_sem=recv,
        device_id=(row, col), device_id_type=MESH,
    )


def down(vector, width):
    return jnp.broadcast_to(vector, (width, vector.shape[1])).T


def gather_kernel(
    x_ref, gain_ref, shift_ref, w1_ref, b1_ref, w2_ref, b2_ref,
    lt_ref, rt_ref,
    own, stage,
    l_send, l_fwd, l_recv, s_send, s_recv, r_send, r_recv,
):
    row, col, x, y, z, k = place()
    home = x // 2
    barrier = pltpu.get_barrier_semaphore()

    def greet(r, c):
        pl.semaphore_signal(barrier, inc=1, device_id=(r, c), device_id_type=MESH)

    for dz in range(1, NZ):
        greet(row, lax.rem(z + dz, NZ) * NK + k)
    greet(row, z * NK + 1 - k)
    for dz in range(1, NZ):
        greet(z * NX + x, lax.rem(z + dz, NZ) * NK + k)

    @pl.when(y != z)
    def _():
        greet(z * NX + x, z * NK + k)

    for xx in range(2):
        for kk in range(NK):
            @pl.when(jnp.logical_or(2 * k + xx != x, kk != k))
            def _(xx=xx, kk=kk):
                greet(y * NX + 2 * k + xx, z * NK + kk)

    gain = down(gain_ref[...], S)
    shift = down(shift_ref[...], S)
    b1 = down(b1_ref[...], S)
    b2 = down(b2_ref[...], S)
    for t in range(2):
        v = x_ref[t].astype(F32)
        mean = jnp.mean(v, axis=0, keepdims=True)
        var = jnp.mean((v - mean) ** 2, axis=0, keepdims=True)
        n = ((v - mean) * lax.rsqrt(var + 1e-05) * gain + shift).astype(BF16)
        own[0, t * C:(t + 1) * C, :] = (
            jnp.dot(w1_ref[...], n, preferred_element_type=F32) + b1
        ).astype(BF16)
        own[1, t * C:(t + 1) * C, :] = (
            jnp.dot(w2_ref[...], n, preferred_element_type=F32) + b2
        ).astype(BF16)

    many = 20 - (y == z).astype(jnp.int32) - (home == k).astype(jnp.int32)
    pl.semaphore_wait(barrier, many)

    def block(ref, index):
        return ref.at[pl.ds(pl.multiple_of(index * OWN, OWN), OWN), :]

    def leg1(dy):
        y2 = lax.rem(y + dy, NY)
        return remote(own.at[1], stage.at[z], s_send.at[dy], s_recv.at[z],
                      y2 * NX + x, y * NK + k)

    def left(dz):
        c2 = lax.rem(z + dz, NZ) * NK + k if dz else z * NK + 1 - k
        return remote(own.at[0], block(lt_ref, col), l_send.at[dz], l_recv.at[col], row, c2)

    for dy in range(1, NY):
        leg1(dy).start()

    @pl.when(y != z)
    def _():
        leg1(0).start()

    for dz in range(NZ):
        left(dz).start()

    @pl.when(y == z)
    def _():
        stage[z] = own[1]

    lt_ref[pl.ds(pl.multiple_of(col * OWN, OWN), OWN), :] = own[0]

    def leg2(d, dx):
        slot = lax.rem(y + d, NZ)
        b = (x % 2) * NCOL + slot * NK + k
        return remote(stage.at[slot], block(rt_ref, b), r_send.at[d, dx], r_recv.at[b],
                      y * NX + lax.rem(x + dx, NX), z * NK + home)

    def pass_on(dz):
        c2 = lax.rem(z + dz, NZ) * NK + k
        return remote(block(lt_ref, c2), block(lt_ref, c2), l_fwd.at[dz], l_recv.at[c2],
                      row, z * NK + 1 - k)

    def arrived(ref, sem):
        pltpu.make_async_copy(ref, ref, sem).wait()

    for d in (0, 1, 7, 2, 6, 3, 5, 4):
        slot = lax.rem(y + d, NZ)
        if d == 0:
            @pl.when(y != z)
            def _():
                arrived(stage.at[slot], s_recv.at[slot])
        else:
            arrived(stage.at[slot], s_recv.at[slot])
        for dx in range(1, NX):
            leg2(d, dx).start()

        @pl.when(home != k)
        def _():
            leg2(d, 0).start()

        @pl.when(home == k)
        def _():
            b = (x % 2) * NCOL + slot * NK + k
            rt_ref[pl.ds(pl.multiple_of(b * OWN, OWN), OWN), :] = stage[slot]

        if d:
            c2 = lax.rem(z + d, NZ) * NK + k
            arrived(block(lt_ref, c2), l_recv.at[c2])
            pass_on(d).start()

    for zz in range(NZ):
        c2 = zz * NK + 1 - k
        arrived(block(lt_ref, c2), l_recv.at[c2])
    for xx in range(2):
        for kk in range(NK):
            @pl.when(jnp.logical_or(2 * k + xx != x, kk != k))
            def _(xx=xx, kk=kk):
                for zz in range(NZ):
                    b = xx * NCOL + zz * NK + kk
                    arrived(block(rt_ref, b), r_recv.at[b])

    for d in range(NY):
        left(d).wait_send()
        if d:
            leg1(d).wait_send()
            pass_on(d).wait_send()
        for dx in range(1, NX):
            leg2(d, dx).wait_send()

    @pl.when(y != z)
    def _():
        leg1(0).wait_send()

    @pl.when(home != k)
    def _():
        for d in range(NY):
            leg2(d, 0).wait_send()


def tile_kernel(
    pairs_ref, lab_ref, labs_ref, bias_ref, cross_ref, w_ref, adj_ref, lt_ref, rt_ref,
    out_ref, lg_ref, rg_ref,
    wide, wf, acc, rtp, lhs, og, fa,
):
    row, col, x, y, z, k = place()
    keep = jnp.int32(0)
    for n in range(pairs_ref.shape[1]):
        hit = jnp.logical_and(pairs_ref[0, n] == row * TI // BLK, pairs_ref[1, n] == col * TJ // BLK)
        keep = jnp.where(hit, jnp.int32(1), keep)
    listed = keep.astype(F32)

    wf[...] = w_ref[...].astype(F32)
    wide[...] = jnp.zeros_like(wide)

    @pl.loop(0, C)
    def _(e):
        we = wf[pl.ds(e, C, stride=C), :].astype(BF16)
        for a in range(G):
            wide[pl.ds(pl.multiple_of(e * G * C + a * C, C), C), a * PW:(a + 1) * PW] = we

    for i in range(TI):
        lhs[(i // G) * TJ:(i // G + 1) * TJ, (i % G) * PW:(i % G + 1) * PW] = (
            adj_ref[i].astype(F32) * listed
        ).astype(BF16)

    @pl.loop(0, C // 4)
    def _(n):
        part = lax.dot_general(
            lhs[...], wide[pl.ds(pl.multiple_of(n * 512, 512), 512), :],
            (((1,), (1,)), ((), ())), preferred_element_type=F32,
        ).astype(BF16)
        for q in range(4):
            for g in range(NG):
                og[pl.ds(pl.multiple_of((n * 4 + q) * TJ, TJ), TJ), g * 128:(g + 1) * 128] = (
                    part[g * TJ:(g + 1) * TJ, q * 128:(q + 1) * 128]
                )

    acc[...] = rt_ref[...].astype(F32)

    @pl.loop(0, C)
    def _(e):
        rtp[pl.ds(pl.multiple_of(e * TJ, TJ), TJ), :] = acc[pl.ds(e, TJ, stride=C), :].astype(BF16)

    @pl.loop(0, 4)
    def _(n):
        rows = pl.ds(pl.multiple_of(n * 512, 512), 512)
        acc[rows, :] = jnp.dot(og[rows, :], lt_ref[...], preferred_element_type=F32) * (1.0 / S)

    @pl.loop(0, TJ)
    def _(j):
        rg_ref[pl.ds(pl.multiple_of(j * C, C), C), :] = acc[pl.ds(j, C, stride=TJ), :].astype(BF16)

    r2 = rtp[...].T
    for n in range(4):
        part = jnp.dot(r2, og[:, n * 256:(n + 1) * 256], preferred_element_type=F32) * (1.0 / S)
        lg_ref[n * 256:(n + 1) * 256, :] = part.T.astype(BF16)

    left = lt_ref[...].T

    @pl.loop(0, C // 4)
    def _(n):
        part = (jnp.dot(
            rtp[pl.ds(pl.multiple_of(n * 256, 256), 256), :], left, preferred_element_type=F32,
        ) * (1.0 / S)).astype(BF16)
        for q in range(4):
            for g in range(NG):
                fa[g * TJ:(g + 1) * TJ, pl.ds(pl.multiple_of((n * 4 + q) * 128, 128), 128)] = (
                    part[q * TJ:(q + 1) * TJ, g * 128:(g + 1) * 128]
                )

    labels = down(lab_ref[pl.ds(z, 1), :], PW)
    mine = jnp.where(k == 0, labels[:TJ], labels[TJ:])
    bias = bias_ref[...] * listed
    cross = cross_ref[...] * listed

    @pl.loop(0, NG)
    def _(g):
        part = jnp.dot(
            fa[pl.ds(pl.multiple_of(g * TJ, TJ), TJ), :], wide[...], preferred_element_type=F32,
        )
        for a in range(G):
            i = g * G + a
            apart = (mine != labs_ref[row * TI + i]).astype(F32)
            out_ref[i] = (
                part[:, a * PW:(a + 1) * PW] * listed + bias + cross * apart
            ).astype(BF16)


def reduce_kernel(
    lg_ref, rg_ref, left_ref, right_ref,
    lx, rx, ry, ys,
    l_send, l_recv, x_send, x_recv, y_send, y_recv,
):
    row, col, x, y, z, k = place()
    barrier = pltpu.get_barrier_semaphore()

    def greet(r, c):
        pl.semaphore_signal(barrier, inc=1, device_id=(r, c), device_id_type=MESH)

    for dx in range(1, NX):
        greet(y * NX + lax.rem(x + dx, NX), col)
    for dy in range(1, NY):
        greet(lax.rem(y + dy, NY) * NX + x, col)
    for dc in range(1, NCOL):
        greet(row, lax.rem(col + dc, NCOL))
    pl.semaphore_wait(barrier, NX - 1 + NY - 1 + NCOL - 1)

    def along_x(dy, dx):
        y2, x2 = lax.rem(y + dy, NY), lax.rem(x + dx, NX)
        return remote(rg_ref.at[y2 * NX + x2], rx.at[dx - 1, dy], x_send.at[dx - 1, dy],
                      x_recv.at[dx - 1, dy], y * NX + x2, col)

    def along_y(dy):
        return remote(ys.at[dy - 1], ry.at[dy - 1], y_send.at[dy - 1], y_recv.at[dy - 1],
                      lax.rem(y + dy, NY) * NX + x, col)

    def along_col(dc):
        c2 = lax.rem(col + dc, NCOL)
        return remote(lg_ref.at[c2], lx.at[dc - 1], l_send.at[dc - 1], l_recv.at[dc - 1], row, c2)

    order = (4, 3, 5, 2, 6, 1, 7, 0)
    for dy in order:
        for dx in range(1, NX):
            along_x(dy, dx).start()
    for dc in range(1, NCOL):
        along_col(dc).start()

    for dy in order:
        total = rg_ref[lax.rem(y + dy, NY) * NX + x].astype(F32)
        for dx in range(1, NX):
            along_x(dy, dx).wait_recv()
            total = total + rx[dx - 1, dy].astype(F32)
        if dy:
            ys[dy - 1] = total.astype(BF16)
            along_y(dy).start()
        else:
            right_ref[...] = total

    total = lg_ref[col].astype(F32)
    for dc in range(1, NCOL):
        along_col(dc).wait_recv()
        total = total + lx[dc - 1].astype(F32)
    left_ref[...] = total

    total = right_ref[...]
    for dy in range(1, NY):
        along_y(dy).wait_recv()
        total = total + ry[dy - 1].astype(F32)
    right_ref[...] = total

    for dy in range(NY):
        for dx in range(1, NX):
            along_x(dy, dx).wait_send()
        if dy:
            along_y(dy).wait_send()
    for dc in range(1, NCOL):
        along_col(dc).wait_send()


def vmem():
    return pl.BlockSpec(memory_space=pltpu.VMEM)


def smem():
    return pl.BlockSpec(memory_space=pltpu.SMEM)


def per_device(
    sequence_features, standardize_scale, standardize_shift,
    first_projection_kernel, first_projection_shift,
    second_projection_kernel, second_projection_shift,
    final_projection_kernel, final_projection_shift, cross_molecule_shift,
    residue_molecule_label, selected_tile_couples, result_adjoint,
):
    dma = pltpu.SemaphoreType.DMA
    lt, rt = pl.pallas_call(
        gather_kernel,
        out_shape=(
            jax.ShapeDtypeStruct((TI * C, S), BF16),
            jax.ShapeDtypeStruct((TJ * C, S), BF16),
        ),
        in_specs=[vmem()] * 7,
        out_specs=(vmem(), vmem()),
        scratch_shapes=[
            pltpu.VMEM((2, OWN, S), BF16),
            pltpu.VMEM((NZ, OWN, S), BF16),
            dma((NZ,)), dma((NZ,)), dma((NCOL,)),
            dma((NY,)), dma((NZ,)),
            dma((NY, NX)), dma((2 * NCOL,)),
        ],
        compiler_params=pltpu.CompilerParams(
            collective_id=0, has_side_effects=True, vmem_limit_bytes=16 * 2**20
        ),
        name="gather_factors",
    )(
        sequence_features.transpose(1, 2, 0),
        standardize_scale[None], standardize_shift[None],
        first_projection_kernel.T, first_projection_shift[None],
        second_projection_kernel.T, second_projection_shift[None],
    )

    pair, lg, rg = pl.pallas_call(
        tile_kernel,
        out_shape=(
            jax.ShapeDtypeStruct((TI, TJ, PW), BF16),
            jax.ShapeDtypeStruct((TI * C, S), BF16),
            jax.ShapeDtypeStruct((TJ * C, S), BF16),
        ),
        in_specs=[smem(), vmem(), smem()] + [vmem()] * 6,
        out_specs=(vmem(), vmem(), vmem()),
        scratch_shapes=[
            pltpu.VMEM((C * G * C, G * PW), BF16),
            pltpu.VMEM((C * C, PW), F32),
            pltpu.VMEM((TJ * C, S), F32),
            pltpu.VMEM((TJ * C, S), BF16),
            pltpu.VMEM((NG * TJ, G * PW), BF16),
            pltpu.VMEM((C * TJ, TI * C), BF16),
            pltpu.VMEM((NG * TJ, C * G * C), BF16),
        ],
        compiler_params=pltpu.CompilerParams(vmem_limit_bytes=48 * 2**20),
        name="pair_tile",
    )(
        selected_tile_couples.T, residue_molecule_label.reshape(8, 128), residue_molecule_label,
        final_projection_shift[None], cross_molecule_shift[None],
        final_projection_kernel, result_adjoint, lt, rt,
    )

    left, right = pl.pallas_call(
        reduce_kernel,
        out_shape=(
            jax.ShapeDtypeStruct((OWN, S), F32),
            jax.ShapeDtypeStruct((OWN, S), F32),
        ),
        in_specs=[vmem()] * 2,
        out_specs=(vmem(), vmem()),
        scratch_shapes=[
            pltpu.VMEM((NCOL - 1, OWN, S), BF16),
            pltpu.VMEM((NX - 1, NY, OWN, S), BF16),
            pltpu.VMEM((NY - 1, OWN, S), BF16),
            pltpu.VMEM((NY - 1, OWN, S), BF16),
            dma((NCOL - 1,)), dma((NCOL - 1,)),
            dma((NX - 1, NY)), dma((NX - 1, NY)),
            dma((NY - 1,)), dma((NY - 1,)),
        ],
        compiler_params=pltpu.CompilerParams(
            collective_id=1, has_side_effects=True, vmem_limit_bytes=16 * 2**20
        ),
        name="reduce_gradients",
    )(lg.reshape(NCOL, OWN, S), rg.reshape(NX * NY, OWN, S))

    def back(grad):
        return grad.reshape(2, C, S).transpose(2, 0, 1)

    return pair, back(left), back(right)


def solution(mesh):
    placed = (P(None, ("row", "col"), None),) + (P(),) * 11 + (P("row", "col", None),)
    return jax.shard_map(
        per_device,
        mesh=mesh,
        in_specs=placed,
        out_specs=(
            P("row", "col", None),
            P(None, ("row", "col"), None),
            P(None, ("col", "row"), None),
        ),
        check_vma=False,
    )
```

time: 535 us -> 73.7 us (0.14)
  waiting for transfers between devices: 407 us -> 0 us
  Pallas kernels: 0 us -> 67 us
  matrix products: 45.4 us -> 0 us
  blocking collectives: 41.7 us -> 0 us
  between operations: 13.8 us -> 0.74 us
  local copies, waits for them, and re-layouts: 16.1 us -> 5.35 us
    reduce_scatter x2 -> x0, waiting for transfers between devices: 276 us -> none  [the longest x1 220 us: per_device(): lax.psum_scatter(right_acc, 'row', scatter_dimension=1, tiled=True)]
    psum x1 -> x0, waiting for transfers between devices: 130 us -> none  [from_root(): return lax.psum(jnp.where(mine, array, jnp.zeros_like(array)), axis)]
    pallas_call x0 -> x3, Pallas kernels: none -> 67 us  [the longest x1 25.7 us: per_device(): pl.pallas_call(gather_kernel, out_shape=(jax.ShapeDtypeStruct((TI * C, S)...]
    dot_general x23 -> x0, matrix products: 45.4 us -> none  [the longest x4 12.7 us: row_step(): jnp.einsum('ijce,sje->sic', outer_grad, right_cols, preferred_element_typ...]
    all_gather x2 -> x0, blocking collectives: 41.7 us -> none  [the longest x1 25.2 us: per_device(): lax.all_gather(right_own, 'col', axis=1, tiled=True)]
    convert_element_type x8 -> x0, local copies, waits for them, and re-layouts: 7.56 us -> none  [the longest x4 4.29 us: row_step(): outer_grad = (outer_grad.reshape(RB, block_column_tokens, factor_matrix *...]
  transfers between devices with their start and end apart: 3 -> 0, of which waited for: 3 -> 0; matrix products, arithmetic and copies ran while one was open for 1% -> 0% of each run, Pallas kernels for 0% -> 0%
where the time goes in v1:
time: 73.7 us; the launch traced here: 73 us
  Pallas kernels  67 us (91%)
  local copies, waits for them, and re-layouts  5.35 us (7%)
  between operations  0.74 us (1%)
    pallas_call x1, Pallas kernels, per_device(): pl.pallas_call(gather_kernel, out_shape=(jax.ShapeDtypeStruct((TI * C, S)...  25.7 us
    pallas_call x1, Pallas kernels, per_device(): pl.pallas_call(tile_kernel, out_shape=(jax.ShapeDtypeStruct((TI, TJ, PW),...  21.9 us
    pallas_call x1, Pallas kernels, per_device(): pl.pallas_call(reduce_kernel, out_shape=(jax.ShapeDtypeStruct((OWN, S), F...  19.3 us
    unnamed x28, local copies, waits for them, and re-layouts  5.35 us

profile of v1, /device:TPU:1, one launch (start us, length us, event | category | flops | bytes accessed | tf_op | source)
XLA Modules:
  0.0 73.0 jit_solution(11915707158045222803)
XLA Ops:
  0.6 0.0 copy-start.9
  0.6 0.0 copy-start.10
  0.7 0.0 copy-start.5
  0.7 0.0 copy-start.4
  0.7 0.0 copy-start.7
  0.7 0.0 copy-start.8
  0.7 0.6 copy-done.9
  1.3 0.0 copy-done.10
  1.3 0.1 copy-done.5
  1.4 0.0 copy-done.4
  1.4 0.8 %copy-done.2 = bf16[128,2,64]{0,2,1:T(8,128)(2,1)S(1)} copy-done((bf16[128,2,64]{0,2,1:T(8,128)(2,1)S(1)}, bf16[128,2,64]{0,2,1:T(8,128)(2,1)}, u32[]{:S(2)}) %copy-start.2) | copy-done | bytes 32792
  2.1 25.7 %gather_factors.1 = (bf16[1024,128]{1,0:T(8,128)(2,1)S(1)}, bf16[2048,128]{1,0:T(8,128)(2,1)S(1)}) custom-call(bf16[2,64,128]{2,1,0:T(8,128)(2,1)S(1)} %bitcast.21, f32[1,64]{1,0:T(1,128)S(1)} %bitcast.28, f32[1,64]{1,0:T(1,128)S(1)} %bitcast.29, bf16[32,64]{1,0:T(8,128)(2,1)S(1)} %bitcast.25, f32[1,32]{1,0:T(1,128)S(1)} %bitcast.30, ...), custom_call_target="tpu_custom_call" | custom-call | tf_op jit(solution)/shard_map/gather_factors/pallas_call | solution.py:361
  27.9 0.0 copy-start.12
  27.9 0.0 copy-start.6
  27.9 0.0 copy-start.11
  27.9 0.0 copy-done.3
  27.9 0.6 copy-done.12
  28.5 0.0 copy-done.6
  28.6 1.0 %copy-done = bf16[32,64,128]{2,1,0:T(8,128)(2,1)S(1)} copy-done((bf16[32,64,128]{2,1,0:T(8,128)(2,1)S(1)}, bf16[32,64,128]{2,1,0:T(8,128)(2,1)}, u32[]{:S(2)}) %copy-start) | copy-done | bytes 524312
  29.6 0.9 %copy-done.1 = bf16[1024,128]{1,0:T(8,128)(2,1)S(1)} copy-done((bf16[1024,128]{1,0:T(8,128)(2,1)S(1)}, bf16[1024,128]{1,0:T(8,128)(2,1)}, u32[]{:S(2)}) %copy-start.1) | copy-done | bytes 262168
  30.5 21.9 %pair_tile.1 = (bf16[32,64,128]{2,1,0:T(8,128)(2,1)}, bf16[1024,128]{1,0:T(8,128)(2,1)S(1)}, bf16[2048,128]{1,0:T(8,128)(2,1)S(1)}) custom-call(s32[2,16]{1,0:T(2,128)S(1)} %bitcast.27, s32[8,128]{1,0:T(8,128)S(1)} %bitcast.24, s32[1024]{0:T(1024)S(1)} %copy-done.3, f32[1,128]{1,0:T(1,128)S(1)} %bitcast.32, f32[1,128]{1,0:T(1,128)S(1)} %bitcast.33, ...), custom_call_target="tpu_custom_call" | custom-call | tf_op jit(solution)/shard_map/pair_tile/pallas_call | solution.py:387
  52.5 19.3 %reduce_gradients.1 = (f32[64,128]{1,0:T(8,128)S(1)}, f32[64,128]{1,0:T(8,128)S(1)}) custom-call(bf16[16,64,128]{2,1,0:T(8,128)(2,1)S(1)} %bitcast.20, bf16[32,64,128]{2,1,0:T(8,128)(2,1)S(1)} %bitcast.19), custom_call_target="tpu_custom_call" | custom-call | tf_op jit(solution)/shard_map/reduce_gradients/pallas_call | solution.py:413
  71.8 0.6 copy.18
  72.4 0.6 copy.19
  (7 shorter events, 0.0 us)
Async XLA Ops:
  0.6 0.7 copy-start.9
  0.6 0.7 copy-start.10
  0.7 0.7 copy-start.5
  0.7 0.7 copy-start.4
  0.7 0.7 copy-start.7
  0.7 0.7 copy-start.8
  1.4 0.8 %copy-start.2 = (bf16[128,2,64]{0,2,1:T(8,128)(2,1)S(1)}, bf16[128,2,64]{0,2,1:T(8,128)(2,1)}, u32[]{:S(2)}) copy-start(bf16[128,2,64]{0,2,1:T(8,128)(2,1)} %param.13) | copy-start | bytes 98308
  2.1 25.7 %copy-start.3 = (s32[1024]{0:T(1024)S(1)}, s32[1024]{0:T(1024)}, u32[]{:S(2)}) copy-start(s32[1024]{0:T(1024)} %labs_ref.1) | copy-start | bytes 12292
  27.9 0.7 copy-start.12
  27.9 0.7 copy-start.6
  27.9 0.7 copy-start.11
  28.6 1.0 %copy-start = (bf16[32,64,128]{2,1,0:T(8,128)(2,1)S(1)}, bf16[32,64,128]{2,1,0:T(8,128)(2,1)}, u32[]{:S(2)}) copy-start(bf16[32,64,128]{2,1,0:T(8,128)(2,1)} %adj_ref.1) | copy-start | bytes 1572868
  29.6 0.9 %copy-start.1 = (bf16[1024,128]{1,0:T(8,128)(2,1)S(1)}, bf16[1024,128]{1,0:T(8,128)(2,1)}, u32[]{:S(2)}) copy-start(bf16[1024,128]{1,0:T(8,128)(2,1)} %w_ref.1) | copy-start | bytes 786436

commit v2 on v0

v2 whole, which is shorter than its diff:
```python
import jax
import jax.numpy as jnp
from jax import lax
from jax.experimental import pallas as pl
from jax.experimental.pallas import tpu as pltpu
from jax.sharding import PartitionSpec as P

F32 = jnp.float32
BF16 = jnp.bfloat16
MESH = pl.DeviceIdType.MESH

NX, NY, NZ, NK = 4, 8, 8, 2
NCOL = NZ * NK
S = 128
C = 32
PW = 128
TI = 32
TJ = 64
OWN = 2 * C
G = 4
NG = TI // G
BLK = 128
FEATURES = 64
LISTED = 16
TOKENS = 1024


def place():
    row, col = lax.axis_index("row"), lax.axis_index("col")
    return row, col, row % NX, row // NX, col // NK, col % NK


def remote(src, dst, send, recv, row, col):
    return pltpu.make_async_remote_copy(
        src_ref=src, dst_ref=dst, send_sem=send, recv_sem=recv,
        device_id=(row, col), device_id_type=MESH,
    )


def down(vector, width):
    return jnp.broadcast_to(vector, (width, vector.shape[1])).T


NEAR = (0, 1, 7, 2, 6, 3, 5, 4)
FAR = (4, 3, 5, 2, 6, 1, 7)
JC = 16


def kernel(
    x_hbm, gain_hbm, shift_hbm, w1_hbm, b1_hbm, w2_hbm, b2_hbm,
    w_hbm, pairs_hbm, adj_hbm, labs_hbm, lab_hbm, bias_hbm, cross_hbm,
    out_ref, grads_ref,
    x_ref, gain_ref, shift_ref, w1_ref, b1_ref, w2_ref, b2_ref,
    w_ref, pairs_ref, adj_ref, labs_ref, lab_ref, bias_ref, cross_ref,
    own, ystage, zstage, lt, rt, wide, wf, acc, rtp, lhs, og, fa,
    lg, rg, lx, rx, ry, ys,
    in_sem, l_send, l_fwd, l_recv, y_send, y_recv, z_send, z_recv, r_send, r_recv,
    lg_send, lg_recv, gx_send, gx_recv, gy_send, gy_recv,
):
    row, col, x, y, z, k = place()
    home = x // 2
    loads = [
        pltpu.make_async_copy(src, dst, in_sem.at[n])
        for n, (src, dst) in enumerate((
            (x_hbm, x_ref), (gain_hbm, gain_ref), (shift_hbm, shift_ref),
            (w1_hbm, w1_ref), (b1_hbm, b1_ref), (w2_hbm, w2_ref), (b2_hbm, b2_ref),
            (w_hbm, w_ref), (pairs_hbm, pairs_ref), (adj_hbm, adj_ref),
            (labs_hbm, labs_ref), (lab_hbm, lab_ref), (bias_hbm, bias_ref), (cross_hbm, cross_ref),
        ))
    ]
    for load in loads:
        load.start()
    barrier = pltpu.get_barrier_semaphore()

    def greet(r, c):
        pl.semaphore_signal(barrier, inc=1, device_id=(r, c), device_id_type=MESH)

    for dc in range(1, NCOL):
        greet(row, lax.rem(col + dc, NCOL))
    for dy in range(1, NY):
        greet(lax.rem(y + dy, NY) * NX + x, col)
    for dx in range(1, NX):
        for kk in range(NK):
            greet(y * NX + lax.rem(x + dx, NX), z * NK + kk)

    for load in loads[:7]:
        load.wait()
    gain = down(gain_ref[...], S)
    shift = down(shift_ref[...], S)
    b1 = down(b1_ref[...], S)
    b2 = down(b2_ref[...], S)
    for t in range(2):
        v = x_ref[t].astype(F32)
        mean = jnp.mean(v, axis=0, keepdims=True)
        var = jnp.mean((v - mean) ** 2, axis=0, keepdims=True)
        n = ((v - mean) * lax.rsqrt(var + 1e-05) * gain + shift).astype(BF16)
        own[0, t * C:(t + 1) * C, :] = (
            jnp.dot(w1_ref[...], n, preferred_element_type=F32) + b1
        ).astype(BF16)
        own[1, t * C:(t + 1) * C, :] = (
            jnp.dot(w2_ref[...], n, preferred_element_type=F32) + b2
        ).astype(BF16)

    wide[...] = jnp.zeros_like(wide)
    loads[7].wait()
    wf[...] = w_ref[...].astype(F32)

    @pl.loop(0, C)
    def _(e):
        we = wf[pl.ds(e, C, stride=C), :].astype(BF16)
        for a in range(G):
            wide[pl.ds(pl.multiple_of(e * G * C + a * C, C), C), a * PW:(a + 1) * PW] = we

    for load in loads[8:]:
        load.wait()
    hits = jnp.int32(0)
    for n in range(pairs_ref.shape[1]):
        hits = hits + (pairs_ref[0, n] == y).astype(jnp.int32) * (
            pairs_ref[1, n] == z
        ).astype(jnp.int32)
    listed = hits.astype(F32)
    for i in range(TI):
        lhs[(i // G) * TJ:(i // G + 1) * TJ, (i % G) * PW:(i % G + 1) * PW] = (
            adj_ref[i].astype(F32) * listed
        ).astype(BF16)

    pl.semaphore_wait(barrier, NCOL - 1 + NY - 1 + NK * (NX - 1))

    def block(ref, index):
        return ref.at[pl.ds(pl.multiple_of(index * OWN, OWN), OWN), :]

    def arrived(ref, sem):
        pltpu.make_async_copy(ref, ref, sem).wait()

    def leg_y(d):
        return remote(own.at[1], ystage.at[y], y_send.at[d], y_recv.at[y],
                      lax.rem(y + d, NY) * NX + x, col)

    def leg_z(d):
        y2 = lax.rem(y + d, NY)
        return remote(ystage.at[y2], zstage.at[z], z_send.at[d], z_recv.at[z],
                      row, y2 * NK + k)

    def leg_x(d, dx):
        slot = lax.rem(z + d, NZ)
        b = (x % 2) * NCOL + slot * NK + k
        return remote(zstage.at[slot], block(rt, b), r_send.at[d, dx], r_recv.at[b],
                      y * NX + lax.rem(x + dx, NX), z * NK + home)

    def left(d):
        c2 = lax.rem(z + d, NZ) * NK + k if d else z * NK + 1 - k
        return remote(own.at[0], block(lt, col), l_send.at[d], l_recv.at[col], row, c2)

    def pass_on(d):
        c2 = lax.rem(z + d, NZ) * NK + k
        return remote(block(lt, c2), block(lt, c2), l_fwd.at[d], l_recv.at[c2],
                      row, z * NK + 1 - k)

    for d in FAR:
        leg_y(d).start()
        left(d).start()
    left(0).start()
    ystage[y] = own[1]
    lt[pl.ds(pl.multiple_of(col * OWN, OWN), OWN), :] = own[0]

    @pl.loop(0, C // 4)
    def _(n):
        part = lax.dot_general(
            lhs[...], wide[pl.ds(pl.multiple_of(n * 512, 512), 512), :],
            (((1,), (1,)), ((), ())), preferred_element_type=F32,
        ).astype(BF16)
        for q in range(4):
            for g in range(NG):
                og[n * 4 + q, :, g * 128:(g + 1) * 128] = (
                    part[g * TJ:(g + 1) * TJ, q * 128:(q + 1) * 128]
                )

    for d in NEAR:
        y2 = lax.rem(y + d, NY)
        if d:
            arrived(ystage.at[y2], y_recv.at[y2])

        @pl.when(y2 != z)
        def _():
            leg_z(d).start()

        @pl.when(y2 == z)
        def _():
            zstage[z] = ystage[z]

    for d in NEAR:
        if d:
            c2 = lax.rem(z + d, NZ) * NK + k
            arrived(block(lt, c2), l_recv.at[c2])
            pass_on(d).start()
    for zz in range(NZ):
        c2 = zz * NK + 1 - k
        arrived(block(lt, c2), l_recv.at[c2])

    def grad_x(y2, dx):
        x2 = lax.rem(x + dx, NX)
        return remote(rg.at[y2 * NX + x2], rx.at[dx - 1, y2], gx_send.at[dx - 1, y2],
                      gx_recv.at[dx - 1, y2], y * NX + x2, col)

    for n in range(TJ // JC):
        acc[...] = jnp.dot(
            og[:, n * JC:(n + 1) * JC, :].reshape(C * JC, TI * C), lt[...],
            preferred_element_type=F32,
        ) * (1.0 / S)
        for j in range(JC):
            at = n * JC + j
            rg[at // 2, (at % 2) * C:(at % 2 + 1) * C, :] = (
                acc[pl.ds(j, C, stride=JC), :].astype(BF16)
            )

    for d in NEAR:
        slot = lax.rem(z + d, NZ)
        if d:
            arrived(zstage.at[slot], z_recv.at[slot])
        for dx in range(1, NX):
            leg_x(d, dx).start()

        @pl.when(home != k)
        def _():
            leg_x(d, 0).start()

        @pl.when(home == k)
        def _():
            b = (x % 2) * NCOL + slot * NK + k
            rt[pl.ds(pl.multiple_of(b * OWN, OWN), OWN), :] = zstage[slot]

    for y2 in range(NY):
        for dx in range(1, NX):
            grad_x(y2, dx).start()

    left_t = lt[...].T
    for xx in range(2):
        for kk in range(NK):
            @pl.when(jnp.logical_or(2 * k + xx != x, kk != k))
            def _(xx=xx, kk=kk):
                for zz in range(NZ):
                    b = xx * NCOL + zz * NK + kk
                    arrived(block(rt, b), r_recv.at[b])

    wide_acc = wf
    for h in range(2):
        wide_acc[...] = rt[h * TI * C:(h + 1) * TI * C, :].astype(F32)
        for e in range(C):
            rtp[e * TJ + h * TI:e * TJ + (h + 1) * TI, :] = (
                wide_acc[pl.ds(e, TI, stride=C), :].astype(BF16)
            )

    right_t = rtp[...].T

    def grad_col(dc):
        c2 = lax.rem(col + dc, NCOL)
        return remote(lg.at[c2], lx.at[dc - 1], lg_send.at[dc - 1], lg_recv.at[dc - 1], row, c2)

    for n in range(4):
        part = jnp.dot(
            right_t, og[:, :, n * 256:(n + 1) * 256].reshape(C * TJ, 256),
            preferred_element_type=F32,
        ) * (1.0 / S)
        lg[n * 4:(n + 1) * 4] = part.T.astype(BF16).reshape(4, OWN, S)
    for dc in range(1, NCOL):
        grad_col(dc).start()

    def grad_y(y2):
        return remote(ys.at[y2], ry.at[y], gy_send.at[y2], gy_recv.at[y], y2 * NX + x, col)

    for y2 in range(NY):
        total = rg[y2 * NX + x].astype(F32)
        for dx in range(1, NX):
            grad_x(y2, dx).wait_recv()
            total = total + rx[dx - 1, y2].astype(F32)

        @pl.when(y2 != y)
        def _():
            ys[y2] = total.astype(BF16)
            grad_y(y2).start()

        @pl.when(y2 == y)
        def _():
            grads_ref[1] = total

    @pl.loop(0, C // 4)
    def _(n):
        part = (jnp.dot(
            rtp[pl.ds(pl.multiple_of(n * 256, 256), 256), :], left_t, preferred_element_type=F32,
        ) * (1.0 / S)).astype(BF16)
        for q in range(4):
            for g in range(NG):
                fa[g * TJ:(g + 1) * TJ, pl.ds(pl.multiple_of((n * 4 + q) * 128, 128), 128)] = (
                    part[q * TJ:(q + 1) * TJ, g * 128:(g + 1) * 128]
                )

    labels = down(lab_ref[pl.ds(z, 1), :], PW)
    mine = jnp.where(k == 0, labels[:TJ], labels[TJ:])
    bias = bias_ref[...] * listed
    cross = cross_ref[...] * listed
    for h in range(2):
        part = jnp.dot(fa[...], wide[:, h * 256:(h + 1) * 256], preferred_element_type=F32)
        for g in range(NG):
            for a in range(2):
                i = g * G + h * 2 + a
                apart = (mine != labs_ref[row * TI + i]).astype(F32)
                out_ref[i] = (
                    part[g * TJ:(g + 1) * TJ, a * PW:(a + 1) * PW] * listed + bias + cross * apart
                ).astype(BF16)

    total = lg[col].astype(F32)
    for dc in range(1, NCOL):
        grad_col(dc).wait_recv()
        total = total + lx[dc - 1].astype(F32)
    grads_ref[0] = total

    total = grads_ref[1]
    for d in range(1, NY):
        y2 = lax.rem(y + d, NY)
        arrived(ry.at[y2], gy_recv.at[y2])
        total = total + ry[y2].astype(F32)
    grads_ref[1] = total

    for d in range(NY):
        left(d).wait_send()
        if d:
            leg_y(d).wait_send()
            pass_on(d).wait_send()
        for dx in range(1, NX):
            leg_x(d, dx).wait_send()
            grad_x(d, dx).wait_send()

        @pl.when(lax.rem(y + d, NY) != z)
        def _():
            leg_z(d).wait_send()

        @pl.when(home != k)
        def _():
            leg_x(d, 0).wait_send()

        @pl.when(d != y)
        def _():
            grad_y(d).wait_send()
    for dc in range(1, NCOL):
        grad_col(dc).wait_send()


def vmem():
    return pl.BlockSpec(memory_space=pltpu.VMEM)


def hbm():
    return pl.BlockSpec(memory_space=pltpu.HBM)


def per_device(
    sequence_features, standardize_scale, standardize_shift,
    first_projection_kernel, first_projection_shift,
    second_projection_kernel, second_projection_shift,
    final_projection_kernel, final_projection_shift, cross_molecule_shift,
    residue_molecule_label, selected_tile_couples, result_adjoint,
):
    dma = pltpu.SemaphoreType.DMA
    block = (OWN, S)
    pair, grads = pl.pallas_call(
        kernel,
        out_shape=(
            jax.ShapeDtypeStruct((TI, TJ, PW), BF16),
            jax.ShapeDtypeStruct((2, OWN, S), F32),
        ),
        in_specs=[hbm()] * 14,
        out_specs=(vmem(), vmem()),
        scratch_shapes=[
            pltpu.VMEM((2, FEATURES, S), BF16),
            pltpu.VMEM((1, FEATURES), F32),
            pltpu.VMEM((1, FEATURES), F32),
            pltpu.VMEM((C, FEATURES), BF16),
            pltpu.VMEM((1, C), F32),
            pltpu.VMEM((C, FEATURES), BF16),
            pltpu.VMEM((1, C), F32),
            pltpu.VMEM((C * C, PW), BF16),
            pltpu.SMEM((2, LISTED), jnp.int32),
            pltpu.VMEM((TI, TJ, PW), BF16),
            pltpu.SMEM((TOKENS,), jnp.int32),
            pltpu.VMEM((NZ, BLK), jnp.int32),
            pltpu.VMEM((1, PW), F32),
            pltpu.VMEM((1, PW), F32),
            pltpu.VMEM((2,) + block, BF16),
            pltpu.VMEM((NY,) + block, BF16),
            pltpu.VMEM((NZ,) + block, BF16),
            pltpu.VMEM((TI * C, S), BF16),
            pltpu.VMEM((TJ * C, S), BF16),
            pltpu.VMEM((C * G * C, G * PW), BF16),
            pltpu.VMEM((C * C, PW), F32),
            pltpu.VMEM((C * JC, S), F32),
            pltpu.VMEM((TJ * C, S), BF16),
            pltpu.VMEM((NG * TJ, G * PW), BF16),
            pltpu.VMEM((C, TJ, TI * C), BF16),
            pltpu.VMEM((NG * TJ, C * G * C), BF16),
            pltpu.VMEM((NCOL,) + block, BF16),
            pltpu.VMEM((NX * NY,) + block, BF16),
            pltpu.VMEM((NCOL - 1,) + block, BF16),
            pltpu.VMEM((NX - 1, NY) + block, BF16),
            pltpu.VMEM((NY,) + block, BF16),
            pltpu.VMEM((NY,) + block, BF16),
            dma((14,)),
            dma((NZ,)), dma((NZ,)), dma((NCOL,)),
            dma((NY,)), dma((NY,)), dma((NY,)), dma((NZ,)),
            dma((NZ, NX)), dma((2 * NCOL,)),
            dma((NCOL - 1,)), dma((NCOL - 1,)),
            dma((NX - 1, NY)), dma((NX - 1, NY)),
            dma((NY,)), dma((NY,)),
        ],
        compiler_params=pltpu.CompilerParams(
            collective_id=0, has_side_effects=True, vmem_limit_bytes=60 * 2**20
        ),
        name="pair_block",
    )(
        sequence_features.transpose(1, 2, 0),
        standardize_scale[None], standardize_shift[None],
        first_projection_kernel.T, first_projection_shift[None],
        second_projection_kernel.T, second_projection_shift[None],
        final_projection_kernel, selected_tile_couples.T, result_adjoint,
        residue_molecule_label, residue_molecule_label.reshape(NZ, BLK),
        final_projection_shift[None], cross_molecule_shift[None],
    )

    def back(grad):
        return grad.reshape(2, C, S).transpose(2, 0, 1)

    return pair, back(grads[0]), back(grads[1])


def solution(mesh):
    placed = (P(None, ("row", "col"), None),) + (P(),) * 11 + (P("row", "col", None),)
    return jax.shard_map(
        per_device,
        mesh=mesh,
        in_specs=placed,
        out_specs=(
            P("row", "col", None),
            P(None, ("row", "col"), None),
            P(None, ("col", "row"), None),
        ),
        check_vma=False,
    )
```

time: 535 us -> 50.4 us (0.09)
  waiting for transfers between devices: 407 us -> 0 us
  Pallas kernels: 0 us -> 46.2 us
  matrix products: 45.4 us -> 0 us
  blocking collectives: 41.7 us -> 0 us
  between operations: 13.8 us -> 0.64 us
  local copies, waits for them, and re-layouts: 16.1 us -> 3.27 us
    reduce_scatter x2 -> x0, waiting for transfers between devices: 276 us -> none  [the longest x1 220 us: per_device(): lax.psum_scatter(right_acc, 'row', scatter_dimension=1, tiled=True)]
    psum x1 -> x0, waiting for transfers between devices: 130 us -> none  [from_root(): return lax.psum(jnp.where(mine, array, jnp.zeros_like(array)), axis)]
    pallas_call x0 -> x1, Pallas kernels: none -> 46.2 us  [per_device(): pl.pallas_call(kernel, out_shape=(jax.ShapeDtypeStruct((TI, TJ, PW), BF16...]
    dot_general x23 -> x0, matrix products: 45.4 us -> none  [the longest x4 12.7 us: row_step(): jnp.einsum('ijce,sje->sic', outer_grad, right_cols, preferred_element_typ...]
    all_gather x2 -> x0, blocking collectives: 41.7 us -> none  [the longest x1 25.2 us: per_device(): lax.all_gather(right_own, 'col', axis=1, tiled=True)]
    convert_element_type x8 -> x0, local copies, waits for them, and re-layouts: 7.56 us -> none  [the longest x4 4.29 us: row_step(): outer_grad = (outer_grad.reshape(RB, block_column_tokens, factor_matrix *...]
  transfers between devices with their start and end apart: 3 -> 0, of which waited for: 3 -> 0; matrix products, arithmetic and copies ran while one was open for 1% -> 0% of each run, Pallas kernels for 0% -> 0%
where the time goes in v2:
time: 50.4 us; the launch traced here: 50.2 us
  Pallas kernels  46.2 us (92%)
  local copies, waits for them, and re-layouts  3.27 us (6%)
  between operations  0.64 us (1%)
    pallas_call x1, Pallas kernels, per_device(): pl.pallas_call(kernel, out_shape=(jax.ShapeDtypeStruct((TI, TJ, PW), BF16...  46.2 us
    unnamed x1, local copies, waits for them, and re-layouts  1.87 us
    slice x1, local copies, waits for them, and re-layouts, per_device(): return (pair, back(grads[0]), back(grads[1]))  1.4 us

profile of v2, /device:TPU:1, one launch (start us, length us, event | category | flops | bytes accessed | tf_op | source)
XLA Modules:
  0.0 50.2 jit_solution(747231276880487515)
XLA Ops:
  0.6 46.2 %pair_block.1 = (bf16[32,64,128]{2,1,0:T(8,128)(2,1)}, f32[2,64,128]{2,1,0:T(8,128)}) custom-call(bf16[2,64,128]{2,1,0:T(8,128)(2,1)} %bitcast.17, f32[1,64]{1,0:T(1,128)} %bitcast.24, f32[1,64]{1,0:T(1,128)} %bitcast.25, bf16[32,64]{1,0:T(8,128)(2,1)} %bitcast.21, f32[1,32]{1,0:T(1,128)} %bitcast.26, bf16[32,64]{1,0:T(8,128)(2,1)} %bitcast.22, ...), custom_call_target="tpu_custom_call" | custom-call | tf_op jit(solution)/shard_map/pair_block/pallas_call | solution.py:365
  46.9 1.4 %fusion = (f32[1,64,128]{2,1,0:T(8,128)}, f32[1,64,128]{2,1,0:T(8,128)}) fusion(f32[2,64,128]{2,1,0:T(8,128)} %get-tuple-element.6), kind=kLoop, calls=%fused_computation | loop fusion | bytes 131072 | tf_op jit(solution)/shard_map/slice | solution.py:431
  48.3 1.9 %copy.17 = bf16[32,64,128]{2,1,0:T(8,128)(2,1)} copy(bf16[32,64,128]{2,1,0:T(8,128)(2,1)} %get-tuple-element.12) | data formatting | bytes 1048576

commit v3 on v2

--- a/solution.py
+++ b/solution.py
@@ -49,12 +49,12 @@
 def kernel(
     x_hbm, gain_hbm, shift_hbm, w1_hbm, b1_hbm, w2_hbm, b2_hbm,
     w_hbm, pairs_hbm, adj_hbm, labs_hbm, lab_hbm, bias_hbm, cross_hbm,
-    out_ref, grads_ref,
+    out_hbm, grads_hbm,
     x_ref, gain_ref, shift_ref, w1_ref, b1_ref, w2_ref, b2_ref,
     w_ref, pairs_ref, adj_ref, labs_ref, lab_ref, bias_ref, cross_ref,
     own, ystage, zstage, lt, rt, wide, wf, acc, rtp, lhs, og, fa,
-    lg, rg, lx, rx, ry, ys,
-    in_sem, l_send, l_fwd, l_recv, y_send, y_recv, z_send, z_recv, r_send, r_recv,
+    lg, rg, lx, rx, ry, ys, pair, sums,
+    in_sem, out_sem, l_send, l_fwd, l_recv, y_send, y_recv, z_send, z_recv, r_send, r_recv,
     lg_send, lg_recv, gx_send, gx_recv, gy_send, gy_recv,
 ):
     row, col, x, y, z, k = place()
@@ -101,6 +101,80 @@
             jnp.dot(w2_ref[...], n, preferred_element_type=F32) + b2
         ).astype(BF16)
 
+    pl.semaphore_wait(barrier, NCOL - 1 + NY - 1 + NK * (NX - 1))
+
+    def block(ref, index):
+        return ref.at[pl.ds(pl.multiple_of(index * OWN, OWN), OWN), :]
+
+    def arrived(ref, sem):
+        pltpu.make_async_copy(ref, ref, sem).wait()
+
+    def leg_y(d):
+        return remote(own.at[1], ystage.at[y], y_send.at[d], y_recv.at[y],
+                      lax.rem(y + d, NY) * NX + x, col)
+
+    def leg_z(d):
+        y2 = lax.rem(y + d, NY)
+        return remote(ystage.at[y2], zstage.at[z], z_send.at[d], z_recv.at[z],
+                      row, y2 * NK + k)
+
+    def leg_x(d, dx):
+        slot = lax.rem(z + d, NZ)
+        b = (x % 2) * NCOL + slot * NK + k
+        return remote(zstage.at[slot], block(rt, b), r_send.at[d, dx], r_recv.at[b],
+                      y * NX + lax.rem(x + dx, NX), z * NK + home)
+
+    def left(d):
+        c2 = lax.rem(z + d, NZ) * NK + k if d else z * NK + 1 - k
+        return remote(own.at[0], block(lt, col), l_send.at[d], l_recv.at[col], row, c2)
+
+    def pass_on(d):
+        c2 = lax.rem(z + d, NZ) * NK + k
+        return remote(block(lt, c2), block(lt, c2), l_fwd.at[d], l_recv.at[c2],
+                      row, z * NK + 1 - k)
+
+    def turn_z(d):
+        y2 = lax.rem(y + d, NY)
+        if d:
+            arrived(ystage.at[y2], y_recv.at[y2])
+
+        @pl.when(y2 != z)
+        def _():
+            leg_z(d).start()
+
+        @pl.when(y2 == z)
+        def _():
+            zstage[z] = ystage[z]
+
+    def turn_x(d):
+        slot = lax.rem(z + d, NZ)
+        if d:
+            arrived(zstage.at[slot], z_recv.at[slot])
+        for dx in range(1, NX):
+            leg_x(d, dx).start()
+
+        @pl.when(home != k)
+        def _():
+            leg_x(d, 0).start()
+
+        @pl.when(home == k)
+        def _():
+            b = (x % 2) * NCOL + slot * NK + k
+            rt[pl.ds(pl.multiple_of(b * OWN, OWN), OWN), :] = zstage[slot]
+
+    def share(d):
+        c2 = lax.rem(z + d, NZ) * NK + k
+        arrived(block(lt, c2), l_recv.at[c2])
+        pass_on(d).start()
+
+    for d in FAR:
+        leg_y(d).start()
+        left(d).start()
+    left(0).start()
+    ystage[y] = own[1]
+    lt[pl.ds(pl.multiple_of(col * OWN, OWN), OWN), :] = own[0]
+    turn_z(0)
+
     wide[...] = jnp.zeros_like(wide)
     loads[7].wait()
     wf[...] = w_ref[...].astype(F32)
@@ -124,75 +198,24 @@
             adj_ref[i].astype(F32) * listed
         ).astype(BF16)
 
-    pl.semaphore_wait(barrier, NCOL - 1 + NY - 1 + NK * (NX - 1))
-
-    def block(ref, index):
-        return ref.at[pl.ds(pl.multiple_of(index * OWN, OWN), OWN), :]
-
-    def arrived(ref, sem):
-        pltpu.make_async_copy(ref, ref, sem).wait()
-
-    def leg_y(d):
-        return remote(own.at[1], ystage.at[y], y_send.at[d], y_recv.at[y],
-                      lax.rem(y + d, NY) * NX + x, col)
-
-    def leg_z(d):
-        y2 = lax.rem(y + d, NY)
-        return remote(ystage.at[y2], zstage.at[z], z_send.at[d], z_recv.at[z],
-                      row, y2 * NK + k)
-
-    def leg_x(d, dx):
-        slot = lax.rem(z + d, NZ)
-        b = (x % 2) * NCOL + slot * NK + k
-        return remote(zstage.at[slot], block(rt, b), r_send.at[d, dx], r_recv.at[b],
-                      y * NX + lax.rem(x + dx, NX), z * NK + home)
-
-    def left(d):
-        c2 = lax.rem(z + d, NZ) * NK + k if d else z * NK + 1 - k
-        return remote(own.at[0], block(lt, col), l_send.at[d], l_recv.at[col], row, c2)
-
-    def pass_on(d):
-        c2 = lax.rem(z + d, NZ) * NK + k
-        return remote(block(lt, c2), block(lt, c2), l_fwd.at[d], l_recv.at[c2],
-                      row, z * NK + 1 - k)
-
-    for d in FAR:
-        leg_y(d).start()
-        left(d).start()
-    left(0).start()
-    ystage[y] = own[1]
-    lt[pl.ds(pl.multiple_of(col * OWN, OWN), OWN), :] = own[0]
-
-    @pl.loop(0, C // 4)
-    def _(n):
-        part = lax.dot_general(
-            lhs[...], wide[pl.ds(pl.multiple_of(n * 512, 512), 512), :],
-            (((1,), (1,)), ((), ())), preferred_element_type=F32,
-        ).astype(BF16)
-        for q in range(4):
-            for g in range(NG):
-                og[n * 4 + q, :, g * 128:(g + 1) * 128] = (
-                    part[g * TJ:(g + 1) * TJ, q * 128:(q + 1) * 128]
-                )
-
-    for d in NEAR:
-        y2 = lax.rem(y + d, NY)
-        if d:
-            arrived(ystage.at[y2], y_recv.at[y2])
-
-        @pl.when(y2 != z)
-        def _():
-            leg_z(d).start()
-
-        @pl.when(y2 == z)
-        def _():
-            zstage[z] = ystage[z]
-
-    for d in NEAR:
-        if d:
-            c2 = lax.rem(z + d, NZ) * NK + k
-            arrived(block(lt, c2), l_recv.at[c2])
-            pass_on(d).start()
+    def outer_grad(first, last):
+        @pl.loop(first, last)
+        def _(n):
+            part = lax.dot_general(
+                lhs[...], wide[pl.ds(pl.multiple_of(n * 512, 512), 512), :],
+                (((1,), (1,)), ((), ())), preferred_element_type=F32,
+            ).astype(BF16)
+            for q in range(4):
+                for g in range(NG):
+                    og[n * 4 + q, :, g * 128:(g + 1) * 128] = (
+                        part[g * TJ:(g + 1) * TJ, q * 128:(q + 1) * 128]
+                    )
+
+    outer_grad(0, 8)
+    for d in NEAR[1:]:
+        turn_z(d)
+    for d in NEAR[1:]:
+        share(d)
     for zz in range(NZ):
         c2 = zz * NK + 1 - k
         arrived(block(lt, c2), l_recv.at[c2])
@@ -214,21 +237,7 @@
             )
 
     for d in NEAR:
-        slot = lax.rem(z + d, NZ)
-        if d:
-            arrived(zstage.at[slot], z_recv.at[slot])
-        for dx in range(1, NX):
-            leg_x(d, dx).start()
-
-        @pl.when(home != k)
-        def _():
-            leg_x(d, 0).start()
-
-        @pl.when(home == k)
-        def _():
-            b = (x % 2) * NCOL + slot * NK + k
-            rt[pl.ds(pl.multiple_of(b * OWN, OWN), OWN), :] = zstage[slot]
-
+        turn_x(d)
     for y2 in range(NY):
         for dx in range(1, NX):
             grad_x(y2, dx).start()
@@ -242,19 +251,17 @@
                     b = xx * NCOL + zz * NK + kk
                     arrived(block(rt, b), r_recv.at[b])
 
-    wide_acc = wf
     for h in range(2):
-        wide_acc[...] = rt[h * TI * C:(h + 1) * TI * C, :].astype(F32)
+        wf[...] = rt[h * TI * C:(h + 1) * TI * C, :].astype(F32)
         for e in range(C):
             rtp[e * TJ + h * TI:e * TJ + (h + 1) * TI, :] = (
-                wide_acc[pl.ds(e, TI, stride=C), :].astype(BF16)
+                wf[pl.ds(e, TI, stride=C), :].astype(BF16)
             )
 
     right_t = rtp[...].T
 
-    def grad_col(dc):
-        c2 = lax.rem(col + dc, NCOL)
-        return remote(lg.at[c2], lx.at[dc - 1], lg_send.at[dc - 1], lg_recv.at[dc - 1], row, c2)
+    def grad_col(c2):
+        return remote(lg.at[c2], lx.at[col], lg_send.at[c2], lg_recv.at[col], row, c2)
 
     for n in range(4):
         part = jnp.dot(
@@ -262,8 +269,10 @@
             preferred_element_type=F32,
         ) * (1.0 / S)
         lg[n * 4:(n + 1) * 4] = part.T.astype(BF16).reshape(4, OWN, S)
-    for dc in range(1, NCOL):
-        grad_col(dc).start()
+        for c2 in range(4 * n, 4 * n + 4):
+            @pl.when(c2 != col)
+            def _(c2=c2):
+                grad_col(c2).start()
 
     def grad_y(y2):
         return remote(ys.at[y2], ry.at[y], gy_send.at[y2], gy_recv.at[y], y2 * NX + x, col)
@@ -281,7 +290,7 @@
 
         @pl.when(y2 == y)
         def _():
-            grads_ref[1] = total
+            sums[1] = total
 
     @pl.loop(0, C // 4)
     def _(n):
@@ -304,22 +313,29 @@
             for a in range(2):
                 i = g * G + h * 2 + a
                 apart = (mine != labs_ref[row * TI + i]).astype(F32)
-                out_ref[i] = (
+                pair[i] = (
                     part[g * TJ:(g + 1) * TJ, a * PW:(a + 1) * PW] * listed + bias + cross * apart
                 ).astype(BF16)
 
+    pair_copy = pltpu.make_async_copy(pair, out_hbm, out_sem.at[0])
+    pair_copy.start()
+
     total = lg[col].astype(F32)
-    for dc in range(1, NCOL):
-        grad_col(dc).wait_recv()
-        total = total + lx[dc - 1].astype(F32)
-    grads_ref[0] = total
-
-    total = grads_ref[1]
+    for d in range(1, NCOL):
+        c2 = lax.rem(col + d, NCOL)
+        arrived(lx.at[c2], lg_recv.at[c2])
+        total = total + lx[c2].astype(F32)
+    sums[0] = total
+
+    total = sums[1]
     for d in range(1, NY):
         y2 = lax.rem(y + d, NY)
         arrived(ry.at[y2], gy_recv.at[y2])
         total = total + ry[y2].astype(F32)
-    grads_ref[1] = total
+    sums[1] = total
+
+    sums_copy = pltpu.make_async_copy(sums, grads_hbm, out_sem.at[1])
+    sums_copy.start()
 
     for d in range(NY):
         left(d).wait_send()
@@ -341,12 +357,29 @@
         @pl.when(d != y)
         def _():
             grad_y(d).wait_send()
-    for dc in range(1, NCOL):
-        grad_col(dc).wait_send()
-
-
-def vmem():
-    return pl.BlockSpec(memory_space=pltpu.VMEM)
+    for c2 in range(NCOL):
+        @pl.when(c2 != col)
+        def _(c2=c2):
+            grad_col(c2).wait_send()
+    pair_copy.wait()
+    sums_copy.wait()
+
+
+def hand_over(pair_in, grads_in, pair_out, left_out, right_out, pair, grads, sems):
+    rows = TI // 4
+    moves = [(grads_in.at[n], grads.at[n], out) for n, out in enumerate((left_out, right_out))] + [
+        (pair_in.at[part], pair.at[part], pair_out.at[part])
+        for part in (pl.ds(n * rows, rows) for n in range(4))
+    ]
+    ins = [pltpu.make_async_copy(a, b, sems.at[0, n]) for n, (a, b, _) in enumerate(moves)]
+    outs = [pltpu.make_async_copy(b, c, sems.at[1, n]) for n, (_, b, c) in enumerate(moves)]
+    for copy in ins:
+        copy.start()
+    for first, then in zip(ins, outs):
+        first.wait()
+        then.start()
+    for copy in outs:
+        copy.wait()
 
 
 def hbm():
@@ -369,7 +402,7 @@
             jax.ShapeDtypeStruct((2, OWN, S), F32),
         ),
         in_specs=[hbm()] * 14,
-        out_specs=(vmem(), vmem()),
+        out_specs=(hbm(), hbm()),
         scratch_shapes=[
             pltpu.VMEM((2, FEATURES, S), BF16),
             pltpu.VMEM((1, FEATURES), F32),
@@ -399,15 +432,17 @@
             pltpu.VMEM((NG * TJ, C * G * C), BF16),
             pltpu.VMEM((NCOL,) + block, BF16),
             pltpu.VMEM((NX * NY,) + block, BF16),
-            pltpu.VMEM((NCOL - 1,) + block, BF16),
+            pltpu.VMEM((NCOL,) + block, BF16),
             pltpu.VMEM((NX - 1, NY) + block, BF16),
             pltpu.VMEM((NY,) + block, BF16),
             pltpu.VMEM((NY,) + block, BF16),
-            dma((14,)),
+            pltpu.VMEM((TI, TJ, PW), BF16),
+            pltpu.VMEM((2,) + block, F32),
+            dma((14,)), dma((2,)),
             dma((NZ,)), dma((NZ,)), dma((NCOL,)),
             dma((NY,)), dma((NY,)), dma((NY,)), dma((NZ,)),
             dma((NZ, NX)), dma((2 * NCOL,)),
-            dma((NCOL - 1,)), dma((NCOL - 1,)),
+            dma((NCOL,)), dma((NCOL,)),
             dma((NX - 1, NY)), dma((NX - 1, NY)),
             dma((NY,)), dma((NY,)),
         ],
@@ -425,10 +460,28 @@
         final_projection_shift[None], cross_molecule_shift[None],
     )
 
+    pair, left, right = pl.pallas_call(
+        hand_over,
+        out_shape=(
+            jax.ShapeDtypeStruct((TI, TJ, PW), BF16),
+            jax.ShapeDtypeStruct(block, F32),
+            jax.ShapeDtypeStruct(block, F32),
+        ),
+        in_specs=[hbm()] * 2,
+        out_specs=(hbm(),) * 3,
+        scratch_shapes=[
+            pltpu.VMEM((TI, TJ, PW), BF16),
+            pltpu.VMEM((2,) + block, F32),
+            dma((2, 6)),
+        ],
+        compiler_params=pltpu.CompilerParams(vmem_limit_bytes=60 * 2**20),
+        name="hand_over",
+    )(pair, grads)
+
     def back(grad):
         return grad.reshape(2, C, S).transpose(2, 0, 1)
 
-    return pair, back(grads[0]), back(grads[1])
+    return pair, back(left), back(right)
 
 
 def solution(mesh):

time: 50.4 us -> 49.5 us (0.982)
  local copies, waits for them, and re-layouts: 3.27 us -> 0 us
  Pallas kernels: 46.2 us -> 48.7 us
    pallas_call x0 -> x1, Pallas kernels: none -> 1.89 us  [per_device(): pl.pallas_call(hand_over, out_shape=(jax.ShapeDtypeStruct((TI, TJ, PW), B...]
    unnamed x1 -> x0, local copies, waits for them, and re-layouts: 1.87 us -> none
    slice x1 -> x0, local copies, waits for them, and re-layouts: 1.4 us -> none  [per_device(): return (pair, back(grads[0]), back(grads[1]))]
    pallas_call x1, Pallas kernels: 46.2 us -> 46.8 us  [per_device(): pl.pallas_call(kernel, out_shape=(jax.ShapeDtypeStruct((TI, TJ, PW), BF16...]
where the time goes in v3:
time: 49.5 us; the launch traced here: 49.4 us
  Pallas kernels  48.7 us (98%)
  between operations  0.64 us (1%)
    pallas_call x1, Pallas kernels, per_device(): pl.pallas_call(kernel, out_shape=(jax.ShapeDtypeStruct((TI, TJ, PW), BF16...  46.8 us
    pallas_call x1, Pallas kernels, per_device(): pl.pallas_call(hand_over, out_shape=(jax.ShapeDtypeStruct((TI, TJ, PW), B...  1.89 us

profile of v3, /device:TPU:1, one launch (start us, length us, event | category | flops | bytes accessed | tf_op | source)
XLA Modules:
  0.0 49.4 jit_solution(14079807988883698226)
XLA Ops:
  0.6 46.8 %pair_block.1 = (bf16[32,64,128]{2,1,0:T(8,128)(2,1)}, f32[2,64,128]{2,1,0:T(8,128)}) custom-call(bf16[2,64,128]{2,1,0:T(8,128)(2,1)} %bitcast.17, f32[1,64]{1,0:T(1,128)} %bitcast.22, f32[1,64]{1,0:T(1,128)} %bitcast.23, bf16[32,64]{1,0:T(8,128)(2,1)} %bitcast.19, f32[1,32]{1,0:T(1,128)} %bitcast.24, bf16[32,64]{1,0:T(8,128)(2,1)} %bitcast.20, ...), custom_call_target="tpu_custom_call" | custom-call | tf_op jit(solution)/shard_map/pair_block/pallas_call | solution.py:398
  47.5 1.9 %hand_over.1 = (bf16[32,64,128]{2,1,0:T(8,128)(2,1)}, f32[64,128]{1,0:T(8,128)}, f32[64,128]{1,0:T(8,128)}) custom-call(bf16[32,64,128]{2,1,0:T(8,128)(2,1)} %get-tuple-element.8.pair_in, f32[2,64,128]{2,1,0:T(8,128)} %get-tuple-element.9.grads_in), custom_call_target="tpu_custom_call" | custom-call | tf_op jit(solution)/shard_map/hand_over/pallas_call | solution.py:463

commit v4 on v3

--- a/solution.py
+++ b/solution.py
@@ -59,6 +59,20 @@
 ):
     row, col, x, y, z, k = place()
     home = x // 2
+    barrier = pltpu.get_barrier_semaphore()
+
+    def greet(r, c):
+        pl.semaphore_signal(barrier, inc=1, device_id=(r, c), device_id_type=MESH)
+
+    for d in FAR:
+        greet(lax.rem(y + d, NY) * NX + x, col)
+        for kk in range(NK):
+            greet(row, lax.rem(z + d, NZ) * NK + kk)
+    greet(row, z * NK + 1 - k)
+    for dx in range(1, NX):
+        for kk in range(NK):
+            greet(y * NX + lax.rem(x + dx, NX), z * NK + kk)
+
     loads = [
         pltpu.make_async_copy(src, dst, in_sem.at[n])
         for n, (src, dst) in enumerate((
@@ -70,19 +84,6 @@
     ]
     for load in loads:
         load.start()
-    barrier = pltpu.get_barrier_semaphore()
-
-    def greet(r, c):
-        pl.semaphore_signal(barrier, inc=1, device_id=(r, c), device_id_type=MESH)
-
-    for dc in range(1, NCOL):
-        greet(row, lax.rem(col + dc, NCOL))
-    for dy in range(1, NY):
-        greet(lax.rem(y + dy, NY) * NX + x, col)
-    for dx in range(1, NX):
-        for kk in range(NK):
-            greet(y * NX + lax.rem(x + dx, NX), z * NK + kk)
-
     for load in loads[:7]:
         load.wait()
     gain = down(gain_ref[...], S)

time: 49.5 us -> 49.4 us (level)
  no operation moved by 1% of the time
where the time goes in v4:
time: 49.4 us; the launch traced here: 49.2 us
  Pallas kernels  48.6 us (98%)
  between operations  0.64 us (1%)
    pallas_call x1, Pallas kernels, per_device(): pl.pallas_call(kernel, out_shape=(jax.ShapeDtypeStruct((TI, TJ, PW), BF16...  46.7 us
    pallas_call x1, Pallas kernels, per_device(): pl.pallas_call(hand_over, out_shape=(jax.ShapeDtypeStruct((TI, TJ, PW), B...  1.89 us

profile of v4, /device:TPU:1, one launch (start us, length us, event | category | flops | bytes accessed | tf_op | source)
XLA Modules:
  0.0 49.2 jit_solution(16275532030379981409)
XLA Ops:
  0.6 46.7 %pair_block.1 = (bf16[32,64,128]{2,1,0:T(8,128)(2,1)}, f32[2,64,128]{2,1,0:T(8,128)}) custom-call(bf16[2,64,128]{2,1,0:T(8,128)(2,1)} %bitcast.17, f32[1,64]{1,0:T(1,128)} %bitcast.22, f32[1,64]{1,0:T(1,128)} %bitcast.23, bf16[32,64]{1,0:T(8,128)(2,1)} %bitcast.19, f32[1,32]{1,0:T(1,128)} %bitcast.24, bf16[32,64]{1,0:T(8,128)(2,1)} %bitcast.20, ...), custom_call_target="tpu_custom_call" | custom-call | tf_op jit(solution)/shard_map/pair_block/pallas_call | solution.py:399
  47.3 1.9 %hand_over.1 = (bf16[32,64,128]{2,1,0:T(8,128)(2,1)}, f32[64,128]{1,0:T(8,128)}, f32[64,128]{1,0:T(8,128)}) custom-call(bf16[32,64,128]{2,1,0:T(8,128)(2,1)} %get-tuple-element.8.pair_in, f32[2,64,128]{2,1,0:T(8,128)} %get-tuple-element.9.grads_in), custom_call_target="tpu_custom_call" | custom-call | tf_op jit(solution)/shard_map/hand_over/pallas_call | solution.py:464

commit v5 on v4

--- a/solution.py
+++ b/solution.py
@@ -212,11 +212,11 @@
                         part[g * TJ:(g + 1) * TJ, q * 128:(q + 1) * 128]
                     )
 
-    outer_grad(0, 8)
     for d in NEAR[1:]:
         turn_z(d)
     for d in NEAR[1:]:
         share(d)
+    outer_grad(0, 8)
     for zz in range(NZ):
         c2 = zz * NK + 1 - k
         arrived(block(lt, c2), l_recv.at[c2])

time: 49.4 us -> 50.4 us (1.020)
  Pallas kernels: 48.6 us -> 49.6 us
    pallas_call x1, Pallas kernels: 46.7 us -> 47.7 us  [per_device(): pl.pallas_call(kernel, out_shape=(jax.ShapeDtypeStruct((TI, TJ, PW), BF16...]
where the time goes in v5:
time: 50.4 us; the launch traced here: 50.2 us
  Pallas kernels  49.6 us (98%)
  between operations  0.64 us (1%)
    pallas_call x1, Pallas kernels, per_device(): pl.pallas_call(kernel, out_shape=(jax.ShapeDtypeStruct((TI, TJ, PW), BF16...  47.7 us
    pallas_call x1, Pallas kernels, per_device(): pl.pallas_call(hand_over, out_shape=(jax.ShapeDtypeStruct((TI, TJ, PW), B...  1.89 us

profile of v5, /device:TPU:1, one launch (start us, length us, event | category | flops | bytes accessed | tf_op | source)
XLA Modules:
  0.0 50.2 jit_solution(6243711806111687174)
XLA Ops:
  0.6 47.7 %pair_block.1 = (bf16[32,64,128]{2,1,0:T(8,128)(2,1)}, f32[2,64,128]{2,1,0:T(8,128)}) custom-call(bf16[2,64,128]{2,1,0:T(8,128)(2,1)} %bitcast.17, f32[1,64]{1,0:T(1,128)} %bitcast.22, f32[1,64]{1,0:T(1,128)} %bitcast.23, bf16[32,64]{1,0:T(8,128)(2,1)} %bitcast.19, f32[1,32]{1,0:T(1,128)} %bitcast.24, bf16[32,64]{1,0:T(8,128)(2,1)} %bitcast.20, ...), custom_call_target="tpu_custom_call" | custom-call | tf_op jit(solution)/shard_map/pair_block/pallas_call | solution.py:399
  48.3 1.9 %hand_over.1 = (bf16[32,64,128]{2,1,0:T(8,128)(2,1)}, f32[64,128]{1,0:T(8,128)}, f32[64,128]{1,0:T(8,128)}) custom-call(bf16[32,64,128]{2,1,0:T(8,128)(2,1)} %get-tuple-element.8.pair_in, f32[2,64,128]{2,1,0:T(8,128)} %get-tuple-element.9.grads_in), custom_call_target="tpu_custom_call" | custom-call | tf_op jit(solution)/shard_map/hand_over/pallas_call | solution.py:464
